TPU v7x, 32 devices: a whole 2x2x4 slice. The times are simulated.
32 devices in a mesh: row: 4 (over y, x), col: 8 (over z, core).
Axes of the slice: x: 2, y: 2, z: 4, core: 2. Of those that a mesh axis runs over, the one named last changes fastest.
Arguments:
- trail_grad: float32 [16384, 16384], P('row', 'col'), may hold values from -20 to 20, as said below
- factor_rows: float32 [16384, 768], P('col', 'row'), may hold values from -0.046875 to 0.046875
- factor_top: float32 [768, 768], replicated, may hold values from -1 to 2, as said below
- rows_grad: float32 [16384, 768], P(('row', 'col')), may hold values from -6 to 6
- top_grad: float32 [768, 768], replicated, may hold values from -6 to 6, as said below
Outputs:
- rows_adjoint: float32 [16384, 768], P(('row', 'col'))
- top_adjoint: float32 [768, 768], replicated
Inputs may be any that keep to these rules, and one draw needn't show every extreme that they name: trail_grad is symmetric once both of its orders are reverted. factor_top is lower triangular with its diagonal between 1 and 2. top_grad is lower triangular.
All inputs are finite; a program needn't handle non-finite values.
Results may differ from a plain program's by a relative error of at most 0.0001.
Values sent between devices are 32-bit elements; how exact they have to be, the bound alone decides.
No kernel may reach another device: no remote copies, remote signals or barrier semaphores. Data moves between devices by JAX's collectives and lax.ppermute only.
A program may use at most 128 MiB of HBM per device.

v0:
```python
import jax
import jax.numpy as jnp
from jax import lax
from jax.sharding import PartitionSpec as P

NB = 256
NP = 3
CB = 128


exact_dots = lax.Precision.HIGHEST


def product(left, right):
    return jnp.dot(left, right, precision=exact_dots, preferred_element_type=jnp.float32)


def column_products(left, right):
    return jnp.einsum(
        "ia,ib->ab", left, right, precision=exact_dots, preferred_element_type=jnp.float32
    )


def halve_diagonal(matrix):
    order = matrix.shape[0]
    row_ids = lax.broadcasted_iota(jnp.int32, (order, order), 0)
    col_ids = lax.broadcasted_iota(jnp.int32, (order, order), 1)
    return jnp.where(row_ids > col_ids, matrix, jnp.where(row_ids == col_ids, 0.5 * matrix, 0.0))


def cholesky_adjoint(factor, inverse, gradient):
    inner = halve_diagonal(product(factor.T, gradient))
    middle = product(product(inverse.T, inner), inverse)
    return halve_diagonal(middle + middle.T)


def per_device(trail_grad, factor_rows, factor_top, rows_grad, top_grad):
    row_owner = lax.axis_index("row")
    col_owner = lax.axis_index("col")
    row_owners = lax.axis_size("row")
    col_owners = lax.axis_size("col")
    owned_rows = trail_grad.shape[0]
    tiles_row = owned_rows // CB
    tiles_col = trail_grad.shape[1] // CB
    panel_width = NP * NB
    piece_rows = rows_grad.shape[0]
    panels = lax.all_gather(factor_rows, "row", axis=1, tiled=True)
    global_rows = (
        lax.broadcasted_iota(jnp.int32, (tiles_row, tiles_col), 0) * row_owners + row_owner
    )
    global_cols = (
        lax.broadcasted_iota(jnp.int32, (tiles_row, tiles_col), 1) * col_owners + col_owner
    )
    intersection = (global_rows == global_cols).astype(jnp.float32)
    aligned_rows = jnp.einsum(
        "kq,qtw->ktw",
        intersection,
        panels.reshape(tiles_col, CB, panel_width),
        precision=exact_dots,
        preferred_element_type=jnp.float32,
    ).reshape(owned_rows, panel_width)
    cross_factor = lax.psum_scatter(aligned_rows, "col", scatter_dimension=0, tiled=True)
    row_index = lax.broadcasted_iota(jnp.int32, (panel_width, NB), 0)
    identity = jnp.eye(NB, dtype=jnp.float32)
    adj_here = jnp.zeros((piece_rows, panel_width), jnp.float32)
    adj_top = jnp.zeros((panel_width, panel_width), jnp.float32)
    cross_adjoints = [None] * NP
    ahead_blocks = [None] * NP
    for which_panel in reversed(range(NP)):
        col_start = which_panel * NB
        col_end = col_start + NB
        below_diag = jnp.where(row_index >= col_end, factor_top[:, col_start:col_end], 0.0)
        diag_block = factor_top[col_start:col_end, col_start:col_end]
        inverse = jax.scipy.linalg.solve_triangular(diag_block, identity, lower=True)
        partial_rows = product(trail_grad, panels[:, col_start:col_end])
        summed_rows = lax.psum_scatter(partial_rows, "col", scatter_dimension=0, tiled=True)
        rows_cbar = (
            rows_grad[:, col_start:col_end] - 2.0 * summed_rows - product(adj_here, below_diag)
        )
        later_blocks = []
        later_blocks = [
            ahead_blocks[later_panel][which_panel] for later_panel in range(which_panel + 1, NP)
        ]
        if later_blocks:
            cross_part = jnp.concatenate([jnp.zeros((col_end, NB), jnp.float32)] + later_blocks, 0)
        else:
            cross_part = jnp.zeros((panel_width, NB), jnp.float32)
        top_masked = jnp.where(row_index >= col_end, top_grad[:, col_start:col_end], 0.0)
        top_cbar = top_masked - (product(adj_top + adj_top.T, below_diag) + cross_part)
        rows_adj = product(rows_cbar, inverse)
        top_adj = product(top_cbar, inverse)
        ahead_sum = lax.psum(column_products(rows_adj, cross_factor[:, :col_end]), ("row", "col"))
        diag_sum = ahead_sum[:, col_start:col_end]
        ahead_blocks[which_panel] = [
            ahead_sum[:, earlier * NB : (earlier + 1) * NB] for earlier in range(which_panel)
        ]
        diag_grad = jnp.tril(
            top_grad[col_start:col_end, col_start:col_end]
            - product(top_adj.T, below_diag)
            - diag_sum
        )
        diag_adjoint = cholesky_adjoint(diag_block, inverse, diag_grad)
        cross_adjoints[which_panel] = rows_adj
        adj_here = adj_here.at[:, col_start:col_end].set(rows_adj)
        adj_top = adj_top.at[:, col_start:col_end].set(
            top_adj.at[col_start:col_end].set(diag_adjoint)
        )
    return (adj_here, adj_top)


def solution(mesh):
    placed = (P("row", "col"), P("col", "row"), P(), P(("row", "col"), None), P())
    return jax.shard_map(
        per_device,
        mesh=mesh,
        in_specs=placed,
        out_specs=(P(("row", "col"), None), P()),
        check_vma=False,
    )
```

profile of v0, /device:TPU:0, one launch (start us, length us, event | category | flops | bytes accessed | tf_op | source)
XLA Modules:
  0.0 590.9 jit_solution(10683462170571645230)
XLA Ops:
  7.9 74.8 %all-gather.2.cloned.1.call-done = f32[2048,768]{0,1:T(8,128)} async-done(((f32[2048,192]{0,1:T(8,128)}), f32[2048,768]{0,1:T(8,128)}) %all-gather.2.cloned.1.call-update) | async-done | bytes 6291472 | tf_op jit(solution)/shard_map/all_gather | solution.py:47
  82.7 31.8 %fusion.7 = f32[4096,256]{1,0:T(8,128)} fusion(f32[4096,2048]{1,0:T(8,128)} %param.25, f32[2048,768]{0,1:T(8,128)} %all-gather.2.cloned.1.call-done), kind=kOutput, calls=%fused_computation.14 | convolution fusion | flops 25769803776 | bytes 39845888 | tf_op jit(solution)/shard_map/dot_general | solution.py:15
  115.1 31.8 %fusion.5 = f32[4096,256]{1,0:T(8,128)} fusion(f32[4096,2048]{1,0:T(8,128)} %param.25, f32[2048,768]{0,1:T(8,128)} %all-gather.2.cloned.1.call-done), kind=kOutput, calls=%fused_computation.12 | convolution fusion | flops 25769803776 | bytes 39845888 | tf_op jit(solution)/shard_map/dot_general | solution.py:15
  147.1 31.9 %fusion.3 = f32[4096,256]{1,0:T(8,128)} fusion(f32[4096,2048]{1,0:T(8,128)} %param.25, f32[2048,768]{0,1:T(8,128)} %all-gather.2.cloned.1.call-done), kind=kOutput, calls=%fused_computation.10 | convolution fusion | flops 25769803776 | bytes 39845888 | tf_op jit(solution)/shard_map/dot_general | solution.py:15
  179.3 6.6 %copy.50 = f32[2048,768]{1,0:T(8,128)} copy(f32[2048,768]{0,1:T(8,128)} %all-gather.2.cloned.1.call-done) | data formatting | bytes 12582912 | tf_op jit(solution)/shard_map/all_gather | solution.py:47
  186.0 14.1 %fusion = f32[32,128,768]{2,0,1:T(8,128)} fusion(f32[16,128,768]{2,1,0:T(8,128)} %bitcast.115, s32[32]{0:T(128)S(1)} %multiply_add_fusion.1, s32[16]{0:T(128)S(1)} %multiply_add_fusion), kind=kOutput, calls=%fused_computation.6 | convolution fusion | flops 603980288 | bytes 18874560 | tf_op jit(solution)/shard_map/kq,qtw->ktw/dot_general | solution.py:55
  200.0 16.5 %copy.52 = f32[32,128,768]{2,1,0:T(8,128)} copy(f32[32,128,768]{2,0,1:T(8,128)} %fusion) | data formatting | bytes 25165824 | tf_op jit(solution)/shard_map/kq,qtw->ktw/dot_general | solution.py:55
  216.6 1.6 copy-done
  218.4 4.4 while.15
  219.4 1.3 bitcast_dynamic-update-slice_fusion.6
  221.4 1.3 bitcast_dynamic-update-slice_fusion.6
  222.7 19.7 %custom-call.5 = f32[2,128,128]{1,2,0:T(8,128)S(1)} custom-call(f32[2,128,128]{2,1,0:T(8,128)S(1)} %get-tuple-element.131), custom_call_target="InvertDiagBlocksLowerTriangular" | custom-call | tf_op jit(solution)/shard_map/jit(_solve_triangular)/triangular_solve | solution.py:74
  242.4 3.9 while.16
  243.0 1.4 bitcast_dynamic-update-slice_fusion.7
  245.0 1.4 bitcast_dynamic-update-slice_fusion.7
  246.4 20.3 %custom-call.6 = f32[2,128,128]{1,2,0:T(8,128)} custom-call(f32[2,128,128]{2,1,0:T(8,128)S(1)} %get-tuple-element.132), custom_call_target="InvertDiagBlocksLowerTriangular" | custom-call | tf_op jit(solution)/shard_map/jit(_solve_triangular)/triangular_solve | solution.py:74
  266.7 3.9 while.17
  267.3 1.4 bitcast_dynamic-update-slice_fusion.8
  269.3 1.4 bitcast_dynamic-update-slice_fusion.8
  270.6 20.3 %custom-call.7 = f32[2,128,128]{1,2,0:T(8,128)} custom-call(f32[2,128,128]{2,1,0:T(8,128)S(1)} %get-tuple-element.133), custom_call_target="InvertDiagBlocksLowerTriangular" | custom-call | tf_op jit(solution)/shard_map/jit(_solve_triangular)/triangular_solve | solution.py:74
  297.0 1.9 fusion.31
  298.9 1.2 scatter.34
  300.1 2.7 convolution_subtract_fusion.1
  302.9 2.2 select_dynamic-update-slice_fusion
  305.1 3.2 convolution_subtract_fusion
  308.3 3.3 fusion.30
  311.5 83.6 %reduce-scatter.11.cloned.1.call-done = f32[512,768]{1,0:T(8,128)} async-done(((f32[4096,768]{1,0:T(8,128)}), f32[512,768]{1,0:T(8,128)}) %reduce-scatter.11.cloned.1.call-update) | async-done | bytes 1572880 | tf_op jit(solution)/shard_map/reduce_scatter | solution.py:62
  395.2 3.9 fusion.135
  399.1 1.7 fusion.28
  400.8 1.9 fusion.18
  402.7 2.0 fusion.24
  404.7 129.3 %all-reduce.6.cloned.1.call-done = (f32[256,768]{1,0:T(8,128)}, f32[256,512]{1,0:T(8,128)}, f32[256,256]{1,0:T(8,128)}) async-done(((f32[256,768]{1,0:T(8,128)}, f32[256,512]{1,0:T(8,128)}, f32[256,256]{1,0:T(8,128)}), (f32[256,768]{1,0:T(8,128)}, f32[256,512]{1,0:T(8,128)}, f32[256,256]{1,0:T(8,128)})) %all-reduce.6.cloned.1.call-update) | async-done | bytes 1572880 | tf_op jit(solution)/shard_map/psum | solution.py:92
  534.0 1.9 fusion.134
  535.9 2.8 fusion.15
  540.5 1.1 copy.55
  541.6 1.5 pad_bitcast_fusion
  543.3 1.6 copy-done.1
  544.8 3.3 fusion.11
  549.7 2.5 fusion.16
  556.6 1.6 broadcast_select_fusion
  558.2 1.4 copy.58
  559.6 2.2 copy.59
  561.9 6.2 %fusion.10 = f32[768,256]{1,0:T(8,128)S(1)} fusion(f32[768,768]{0,1:T(8,128)S(1)} %constant_dynamic-update-slice_fusion.1, f32[768,768]{1,0:T(8,128)} %copy.59, f32[256,256]{1,0:T(8,128)S(1)} %copy-done.13, f32[256,256]{1,0:T(8,128)S(1)} %copy-done.12, f32[256,256]{1,0:T(8,128)S(1)} %triangular_solve.91, f32[768,768]{1,0:T(8,128)} %param.29, ...), kind=kOutput, calls=%fused_computation.17 | convolution fusion | flops 1813708800 | bytes 7866368 | tf_op jit(solution)/shard_map/dot_general | solution.py:15
  568.9 1.1 copy.62
  570.0 2.8 fusion.17
  572.9 1.6 convolution_bitcast_fusion
  576.2 1.8 copy.61
  581.7 2.0 copy.64
  (107 shorter events, 25.5 us)
Async XLA Ops:
  7.2 75.6 %all-gather.2.cloned.1.call-start = ((), (), s32[]{:S(2)}) async-start(), calls=%async_computation.4 | async-start | bytes 7864320 | tf_op jit(solution)/shard_map/all_gather | solution.py:47
  7.9 289.1 %reduce-scatter.5.cloned.1.call-start = ((), (), s32[]{:S(2)}) async-start(), calls=%async_computation.5 | async-start | bytes 4718592 | tf_op jit(solution)/shard_map/reduce_scatter | solution.py:76
  114.5 185.6 %reduce-scatter.7.cloned.1.call-start = ((), (), s32[]{:S(2)}) async-start(), calls=%async_computation.6 | async-start | bytes 4718592 | tf_op jit(solution)/shard_map/reduce_scatter | solution.py:76
  146.9 158.2 %reduce-scatter.9.cloned.1.call-start = ((), (), s32[]{:S(2)}) async-start(), calls=%async_computation.7 | async-start | bytes 4718592 | tf_op jit(solution)/shard_map/reduce_scatter | solution.py:76
  179.0 216.1 %reduce-scatter.11.cloned.1.call-start = ((), (), s32[]{:S(2)}) async-start(), calls=%async_computation.8 | async-start | bytes 14155776 | tf_op jit(solution)/shard_map/reduce_scatter | solution.py:62
  216.6 1.7 copy-start
  216.6 317.4 %all-reduce.6.cloned.1.call-start = ((), (), s32[]{:S(2)}) async-start(), calls=%async_computation.9 | async-start | bytes 3145728 | tf_op jit(solution)/shard_map/psum | solution.py:92
  290.9 4.8 copy-start.16
  290.9 5.1 copy-start.17
  296.1 6.8 %copy-start.6 = (f32[128,256]{1,0:T(8,128)}, f32[128,256]{1,0:T(8,128)S(1)}, u32[]{:S(2)}) copy-start(f32[128,256]{1,0:T(8,128)S(1)} %fusion.97) | copy-start | bytes 393220
  297.0 11.3 %copy-start.4 = (f32[128,256]{1,0:T(8,128)}, f32[128,256]{1,0:T(8,128)S(1)}, u32[]{:S(2)}) copy-start(f32[128,256]{1,0:T(8,128)S(1)} %fusion.95) | copy-start | bytes 393220
  395.2 4.0 copy-start.3
  395.2 4.0 copy-start.10
  395.2 5.7 copy-start.11
  534.0 5.3 copy-start.8
  541.6 1.5 copy-start.2
  541.6 1.6 copy-start.14
  543.1 1.7 copy-start.1
  544.8 3.3 copy-start.7
  544.8 4.1 copy-start.15
  559.6 2.2 copy-start.12
  559.6 2.2 copy-start.13
  561.9 6.2 %copy-start.5 = (f32[128,256]{1,0:T(8,128)S(1)}, f32[128,256]{1,0:T(8,128)}, u32[]{:S(2)}) copy-start(f32[128,256]{1,0:T(8,128)} %copy-done.4) | copy-start | bytes 393220
  572.9 7.0 %copy-start.9 = (f32[768,256]{0,1:T(8,128)S(1)}, f32[768,256]{0,1:T(8,128)}, u32[]{:S(2)}) copy-start(f32[768,256]{0,1:T(8,128)} %copy.62) | copy-start | bytes 2359300
Sparse Core Ops, SparseCore 0:
  9.8 72.8 all-gather.1
  114.6 49.9 reduce-scatter.4
  167.0 48.1 reduce-scatter.6
  217.3 48.1 reduce-scatter.8
  267.6 127.4 reduce-scatter.10
  402.8 131.1 all-reduce.5
where the time goes:
time: 597 us; the launch traced here: 591 us
  waiting for transfers between devices  288 us (48%)
  matrix products  163 us (27%)
  other arithmetic  66.7 us (11%)
  local copies, waits for them, and re-layouts  56.2 us (9%)
  between operations  15.1 us (3%)
    dot_general x25, matrix products, product(): jnp.dot(left, right, precision=exact_dots, preferred_element_type=jnp.flo...  137 us
    psum x1, waiting for transfers between devices, per_device(): lax.psum(column_products(rows_adj, cross_factor[:, :col_end]), ('row', 'c...  129 us
    reduce_scatter x1, waiting for transfers between devices, per_device(): lax.psum_scatter(aligned_rows, 'col', scatter_dimension=0, tiled=True)  83.6 us
    all_gather x1, waiting for transfers between devices, per_device(): panels = lax.all_gather(factor_rows, 'row', axis=1, tiled=True)  74.8 us
    another operation x5, other arithmetic, per_device(): jax.scipy.linalg.solve_triangular(diag_block, identity, lower=True)  60.3 us
    dot_general x1, local copies, waits for them, and re-layouts, per_device(): jnp.einsum('kq,qtw->ktw', intersection, panels.reshape(tiles_col, CB, pan...  16.5 us
    dot_general x1, matrix products, per_device(): jnp.einsum('kq,qtw->ktw', intersection, panels.reshape(tiles_col, CB, pan...  14.1 us
  transfers between devices with their start and end apart: 6, of which 3 were waited for; matrix products, arithmetic and copies ran while one was open for 33% of the time, Pallas kernels for 0%

commit v1 on v0

v1 whole, which is shorter than its diff:
```python
import functools

import jax
import jax.numpy as jnp
import numpy as np
from jax import lax
from jax.experimental import pallas as pl
from jax.experimental.pallas import tpu as pltpu
from jax.sharding import PartitionSpec as P

NB = 256
NP = 3
CB = 128
LEAF = 32

exact_dots = lax.Precision.HIGHEST
split_dots = lax.Precision.HIGH


def dims_dot(left, right, left_dim, right_dim, precision=exact_dots):
    return lax.dot_general(
        left,
        right,
        (((left_dim,), (right_dim,)), ((), ())),
        precision=precision,
        preferred_element_type=jnp.float32,
    )


def product(left, right):
    return dims_dot(left, right, 1, 0)


def lower_half(matrix):
    row_ids = lax.broadcasted_iota(jnp.int32, matrix.shape, 0)
    col_ids = lax.broadcasted_iota(jnp.int32, matrix.shape, 1)
    return jnp.where(row_ids > col_ids, matrix, jnp.where(row_ids == col_ids, 0.5 * matrix, 0.0))


def inverse_kernel(leaf_ref, factor_ref, out_ref, leaf_out):
    width = factor_ref.shape[0]
    dot = functools.partial(jnp.dot, precision=exact_dots, preferred_element_type=jnp.float32)
    lane = lax.broadcasted_iota(jnp.int32, (1, width), 1) % LEAF
    row_at = lax.broadcasted_iota(jnp.int32, (LEAF, width), 0)
    leaf_out[...] = jnp.zeros_like(leaf_out)
    for row in range(LEAF):
        known = leaf_ref[row]
        diag = known[row : row + 1]
        total = jnp.sum(jnp.where(row_at < row, known * leaf_out[...], 0.0), axis=0, keepdims=True)
        leaf_out[row : row + 1] = (jnp.where(lane == row, 1.0, 0.0) - total) / diag
    out_ref[...] = jnp.zeros_like(out_ref)
    for at in range(0, width, CB):
        spread = jnp.concatenate([leaf_out[:, at : at + CB]] * (CB // LEAF), 0)
        rows = lax.broadcasted_iota(jnp.int32, (CB, CB), 0)
        cols = lax.broadcasted_iota(jnp.int32, (CB, CB), 1)
        inv = jnp.where(rows // LEAF == cols // LEAF, spread, 0.0)
        block = factor_ref[at : at + CB, at : at + CB]
        size = LEAF
        while size < CB:
            below = (rows // size == cols // size + 1) & (rows // (2 * size) == cols // (2 * size))
            inv = inv - dot(dot(inv, jnp.where(below, block, 0.0)), inv)
            size *= 2
        out_ref[at : at + CB, at : at + CB] = inv
    for at in range(0, width, NB):
        size = CB
        while size < NB:
            for low in range(at, at + NB, 2 * size):
                mid, high = low + size, low + 2 * size
                first = out_ref[low:mid, low:mid]
                second = out_ref[mid:high, mid:high]
                out_ref[mid:high, low:mid] = -dot(dot(second, factor_ref[mid:high, low:mid]), first)
            size *= 2
    for at in range(NB, width, NB):
        carried = dot(factor_ref[at : at + NB, :at], out_ref[:at, :at])
        out_ref[at : at + NB, :at] = -dot(out_ref[at : at + NB, at : at + NB], carried)


def triangular_inverse(factor):
    width = factor.shape[0]
    leaves = width // LEAF
    blocks = jnp.stack(
        [factor[i * LEAF : (i + 1) * LEAF, i * LEAF : (i + 1) * LEAF] for i in range(leaves)], 2
    )
    spread = jnp.repeat(blocks, LEAF, axis=2)
    return pl.pallas_call(
        inverse_kernel,
        out_shape=jax.ShapeDtypeStruct((width, width), jnp.float32),
        in_specs=[pl.BlockSpec(memory_space=pltpu.VMEM)] * 2,
        out_specs=pl.BlockSpec(memory_space=pltpu.VMEM),
        scratch_shapes=[pltpu.VMEM((LEAF, width), jnp.float32)],
        compiler_params=pltpu.CompilerParams(vmem_limit_bytes=32 * 1024 * 1024),
        cost_estimate=pl.CostEstimate(flops=2 * width**3, bytes_accessed=16 * width**2, transcendentals=0),
    )(spread, factor)


def pick(blocks, which):
    return lax.dynamic_index_in_dim(blocks, which, 0, keepdims=False)


def swap(block, axis, offset):
    return lax.ppermute(block, axis, [(i, i ^ offset) for i in range(lax.axis_size(axis))])


def exchange(blocks, axis):
    here = lax.axis_index(axis)
    size = lax.axis_size(axis)
    arrived = [pick(blocks, here)]
    arrived += [swap(pick(blocks, here ^ offset), axis, offset) for offset in range(1, size)]
    stacked = jnp.stack(arrived)
    return [pick(stacked, here ^ i) for i in range(size)]


def align_rows(panel):
    col_owners, row_owners = lax.axis_size("col"), lax.axis_size("row")
    width, owned = panel.shape
    part = owned // col_owners
    pieces = panel.reshape(width, col_owners, part).transpose(1, 0, 2)
    from_cols = exchange(pieces, "col")
    per_row = col_owners // row_owners
    tile = min(CB, part)
    for_rows = []
    for row in range(row_owners):
        parts = [from_cols[each * row_owners + row] for each in range(per_row)]
        cuts = [
            cut[:, at : at + tile] for at in range(0, part, tile) for cut in parts
        ]
        for_rows.append(jnp.concatenate(cuts, 1))
    return jnp.concatenate(exchange(jnp.stack(for_rows), "row"), 0)


def gather_panels(panel):
    row_owners = lax.axis_size("row")
    half = panel.shape[0] // 2
    have = {0: (panel[:half], panel[half:])}
    for offset in range(1, row_owners):
        low = offset & -offset
        high = 1 << (offset.bit_length() - 1)
        have[offset] = (
            swap(have[offset ^ low][0], "row", low),
            swap(have[offset ^ high][1], "row", high),
        )
    return [jnp.concatenate(have[offset], 0) for offset in range(row_owners)]


def sum_over_cols(partial):
    planes = lax.axis_size("col") // 2
    width = partial.shape[0]
    here = lax.axis_index("col")
    plane, core = here // 2, here % 2
    blocks = partial.reshape(width, planes, 2, -1).transpose(2, 1, 0, 3)
    mine = pick(blocks, core) + swap(pick(blocks, 1 - core), "col", 1)
    rising = falling = None
    for hops in range(planes - 1, 0, -1):
        up = pick(mine, jnp.minimum(plane + hops, planes - 1))
        down = pick(mine, jnp.maximum(plane - hops, 0))
        if rising is not None:
            up, down = up + rising, down + falling
        pairs = [(2 * at + k, 2 * at + 2 + k) for at in range(planes - hops) for k in range(2)]
        rising = lax.ppermute(up, "col", pairs)
        falling = lax.ppermute(down, "col", [(2 * planes - 1 - a, 2 * planes - 1 - b) for a, b in pairs])
    return pick(mine, plane) + rising + falling


def sum_everywhere(block, least):
    order = [("col", 1)]
    order += [("row", 1 << b) for b in range(lax.axis_size("row").bit_length() - 1)]
    order += [("col", 1 << b) for b in range(1, lax.axis_size("col").bit_length() - 1)]
    halved = []
    for axis, bit in order:
        rows = block.shape[0]
        if rows // 2 >= least and rows % 16 == 0:
            upper = (lax.axis_index(axis) & bit) != 0
            low, high = block[: rows // 2], block[rows // 2 :]
            block = jnp.where(upper, high, low) + swap(jnp.where(upper, low, high), axis, bit)
            halved.append((axis, bit, upper))
        else:
            block = block + swap(block, axis, bit)
    for axis, bit, upper in reversed(halved):
        other = swap(block, axis, bit)
        block = jnp.concatenate([jnp.where(upper, other, block), jnp.where(upper, block, other)], 0)
    return block


def slot_table(row_owners):
    table = []
    for row in range(row_owners):
        rest = [row ^ (1 << b) for b in range(row_owners.bit_length() - 1)]
        second = max(rest)
        others = [c for c in range(row_owners - 1, -1, -1) if c not in (row, second)]
        table.append([row, second] + others)
    return np.array(table)


def per_device(trail_grad, factor_rows, factor_top, rows_grad, top_grad):
    row_owner = lax.axis_index("row")
    row_owners = lax.axis_size("row")
    panel_width = factor_top.shape[0]
    chunk = factor_rows.shape[1]
    own_panel = factor_rows.T
    table = slot_table(row_owners)
    late = len(set(table[:, -1]))
    split = late * chunk

    panels = gather_panels(own_panel)
    aligned = align_rows(own_panel)
    grad_chunks = rows_grad.T.reshape(row_owners, chunk, -1)
    inverse = triangular_inverse(factor_top)

    adjoint_rows = jnp.zeros_like(grad_chunks)
    inner = jnp.zeros((row_owners, chunk, panel_width), jnp.float32)
    for slot in range(row_owners):
        which = jnp.asarray(table[:, slot])[row_owner]
        offsets = sorted({int(table[r, slot]) ^ r for r in range(row_owners)})
        panel = panels[offsets[0]]
        for offset in offsets[1:]:
            panel = jnp.where((which ^ row_owner) == offset, panels[offset], panel)
        partial = dims_dot(panel, trail_grad, 1, 1, split_dots)
        rest = pick(grad_chunks, which) - 2.0 * sum_over_cols(partial)
        adjoint_rows = lax.dynamic_update_index_in_dim(adjoint_rows, rest, which, 0)
        inner = lax.dynamic_update_index_in_dim(inner, dims_dot(rest, aligned, 1, 1), which, 0)
        if slot == row_owners - 2:
            early = inner[late:].reshape(-1, panel_width)
    early = sum_everywhere(early, 8)
    last = sum_everywhere(inner[:late].reshape(split, panel_width)[:, :split], 64)

    adjoint_rows = adjoint_rows.reshape(panel_width, -1)
    rows_out = dims_dot(adjoint_rows, inverse, 0, 0, split_dots)

    lo, hi = slice(0, split), slice(split, panel_width)
    inv_lo, inv_hi, inv_mix = inverse[lo, lo], inverse[hi, hi], inverse[hi, lo]
    fac_lo, fac_hi, fac_mix = factor_top[lo, lo], factor_top[hi, hi], factor_top[hi, lo]
    moved = dims_dot(inv_hi, early, 0, 0)
    bar_mix = top_grad[hi, lo] - moved[:, lo]
    bar_hi = jnp.tril(top_grad[hi, hi] - moved[:, hi])
    mid_mix = dims_dot(fac_hi, bar_mix, 0, 0)
    mid_hi = lower_half(dims_dot(fac_hi, bar_hi, 0, 0))
    left_mix = dims_dot(inv_hi, mid_mix, 0, 0)
    left_hi = dims_dot(inv_hi, mid_hi, 0, 0)
    left_over = dims_dot(inv_mix, mid_hi, 0, 0)
    out_hi = product(left_hi, inv_hi)
    out_mix = product(left_mix, inv_lo) + product(left_hi, inv_mix) + product(left_over, inv_hi).T
    out_hi = lower_half(out_hi + out_hi.T)
    bar_known = top_grad[lo, lo] - dims_dot(inv_mix, early[:, lo], 0, 0)
    mid_known = dims_dot(fac_mix, bar_mix, 0, 0)
    left_known = dims_dot(inv_mix, mid_mix, 0, 0)
    out_known = product(left_over, inv_mix)

    bar_lo = jnp.tril(bar_known - dims_dot(inv_lo, last, 0, 0))
    mid_lo = lower_half(dims_dot(fac_lo, bar_lo, 0, 0) + mid_known)
    left_lo = dims_dot(inv_lo, mid_lo, 0, 0) + left_known
    out_lo = product(left_lo, inv_lo) + out_known
    out_lo = lower_half(out_lo + out_lo.T)
    top_out = jnp.concatenate(
        [
            jnp.concatenate([out_lo, jnp.zeros_like(out_mix.T)], 1),
            jnp.concatenate([out_mix, out_hi], 1),
        ],
        0,
    )
    return rows_out, top_out


def solution(mesh):
    placed = (P("row", "col"), P("col", "row"), P(), P(("row", "col"), None), P())
    return jax.shard_map(
        per_device,
        mesh=mesh,
        in_specs=placed,
        out_specs=(P(("row", "col"), None), P()),
        check_vma=False,
    )
```

time: 597 us -> 528 us (0.88)
  waiting for transfers between devices: 288 us -> 80.6 us
  starting transfers between devices: 1.15 us -> 120 us
  local copies, waits for them, and re-layouts: 56.2 us -> 149 us
  other arithmetic: 66.7 us -> 21.3 us
  matrix products: 163 us -> 134 us
  Pallas kernels: 0 us -> 6.67 us
    psum x1 -> x0, waiting for transfers between devices: 129 us -> none  [per_device(): lax.psum(column_products(rows_adj, cross_factor[:, :col_end]), ('row', 'c...]
    ppermute x0 -> x60, starting transfers between devices: none -> 120 us  [the longest x12 67.8 us: sum_over_cols(): rising = lax.ppermute(up, 'col', pairs)]
    reduce_scatter x4 -> x0, waiting for transfers between devices: 83.6 us -> none  [the longest x1 83.6 us: per_device(): lax.psum_scatter(aligned_rows, 'col', scatter_dimension=0, tiled=True)]
    ppermute x0 -> x60, waiting for transfers between devices: none -> 80.6 us  [the longest x36 60.5 us: swap(): lax.ppermute(block, axis, [(i, i ^ offset) for i in range(lax.axis_size(a...]
    all_gather x1 -> x0, waiting for transfers between devices: 74.8 us -> none  [per_device(): panels = lax.all_gather(factor_rows, 'row', axis=1, tiled=True)]
    another operation x9 -> x6, other arithmetic: 63.6 us -> 1.59 us  [the longest x1 1.35 us: exchange(): stacked = jnp.stack(arrived)]
    unnamed x37 -> x142, local copies, waits for them, and re-layouts: 5.16 us -> 59.6 us
    reshape x0 -> x5, local copies, waits for them, and re-layouts: none -> 29.3 us  [the longest x4 19.5 us: sum_over_cols(): blocks = partial.reshape(width, planes, 2, -1).transpose(2, 1, 0, 3)]
  transfers between devices with their start and end apart: 6 -> 60, of which waited for: 3 -> 18; matrix products, arithmetic and copies ran while one was open for 33% -> 48% of each run, Pallas kernels for 0% -> 1%
where the time goes in v1:
time: 528 us; the launch traced here: 522 us
  local copies, waits for them, and re-layouts  149 us (28%)
  matrix products  134 us (25%)
  starting transfers between devices  120 us (23%)
  waiting for transfers between devices  80.6 us (15%)
  other arithmetic  21.3 us (4%)
  between operations  10.3 us (2%)
  Pallas kernels  6.67 us (1%)
    dot_general x27, matrix products, dims_dot(): lax.dot_general(left, right, (((left_dim,), (right_dim,)), ((), ())), pre...  134 us
    ppermute x12, starting transfers between devices, sum_over_cols(): rising = lax.ppermute(up, 'col', pairs)  67.8 us
    ppermute x36, waiting for transfers between devices, swap(): lax.ppermute(block, axis, [(i, i ^ offset) for i in range(lax.axis_size(a...  60.5 us
    unnamed x142, local copies, waits for them, and re-layouts  59.6 us
    ppermute x36, starting transfers between devices, swap(): lax.ppermute(block, axis, [(i, i ^ offset) for i in range(lax.axis_size(a...  41.5 us
    another operation x3, local copies, waits for them, and re-layouts  25.7 us
    ppermute x12, waiting for transfers between devices, sum_over_cols(): rising = lax.ppermute(up, 'col', pairs)  20 us
    reshape x4, local copies, waits for them, and re-layouts, sum_over_cols(): blocks = partial.reshape(width, planes, 2, -1).transpose(2, 1, 0, 3)  19.5 us
  transfers between devices with their start and end apart: 60, of which 18 were waited for; matrix products, arithmetic and copies ran while one was open for 48% of the time, Pallas kernels for 1%

profile of v1, /device:TPU:0, one launch (start us, length us, event | category | flops | bytes accessed | tf_op | source)
XLA Modules:
  0.0 521.9 jit_solution(8309545915093310975)
XLA Ops:
  0.6 2.8 fusion.91
  3.4 3.0 collective-permute-start.7
  13.1 22.6 %fusion.100 = f32[192,4096]{1,0:T(8,128)} fusion(f32[2048,192]{0,1:T(8,128)S(1)} %copy-done.3, f32[4096,2048]{1,0:T(8,128)} %param.9), kind=kOutput, calls=%fused_computation.298 | convolution fusion | flops 9663676416 | bytes 38273024 | tf_op jit(solution)/shard_map/dot_general | solution.py:21
  62.5 2.6 collective-permute-start.37
  65.3 3.6 collective-permute-start.39
  68.9 15.2 %collective-permute-done.37 = f32[192,256]{1,0:T(8,128)S(1)} collective-permute-done((f32[192,256]{1,0:T(8,128)}, f32[192,256]{1,0:T(8,128)S(1)}, u32[]{:S(2)}, u32[]{:S(2)}) %collective-permute-start.37) | collective-permute-done | bytes 196640 | tf_op jit(solution)/shard_map/ppermute | solution.py:101
  87.0 5.8 %collective-permute-done.40 = f32[192,256]{1,0:T(8,128)S(1)} collective-permute-done((f32[192,256]{1,0:T(8,128)S(1)}, f32[192,256]{1,0:T(8,128)S(1)}, u32[]{:S(2)}, u32[]{:S(2)}) %collective-permute-start.40) | collective-permute-done | bytes 196640 | tf_op jit(solution)/shard_map/ppermute | solution.py:101
  105.8 3.8 reshape.54
  109.6 3.1 copy.22
  122.6 11.2 %collective-permute-done.8 = f32[96,2048]{1,0:T(8,128)S(1)} collective-permute-done((f32[96,2048]{1,0:T(8,128)}, f32[96,2048]{1,0:T(8,128)S(1)}, u32[]{:S(2)}, u32[]{:S(2)}) %collective-permute-start.8) | collective-permute-done | bytes 786464 | tf_op jit(solution)/shard_map/ppermute | solution.py:101
  133.9 2.5 collective-permute-done.10
  137.3 22.3 %fusion.9 = f32[192,4096]{1,0:T(8,128)} fusion(f32[4096,2048]{1,0:T(8,128)} %param.9, f32[192,2048]{1,0:T(8,128)S(1)} %constant_dynamic-update-slice_fusion, f32[192,2048]{1,0:T(8,128)S(1)} %constant_dynamic-update-slice_fusion.2, pred[]{:T(512)S(6)} %eq.29), kind=kOutput, calls=%fused_computation.25 | convolution fusion | flops 9664069632 | bytes 39845888 | tf_op jit(solution)/shard_map/dot_general | solution.py:21
  159.7 5.8 %reshape.55 = f32[192,4,2,512]{3,2,1,0:T(2,128)} reshape(f32[192,4096]{1,0:T(8,128)} %fusion.9) | data formatting | bytes 6291456 | tf_op jit(solution)/shard_map/reshape | solution.py:150
  167.0 12.8 %constant_dynamic-slice_fusion.32 = (f32[192,4,1,512]{3,2,1,0:T(1,128)}, f32[1,4,192,512]{3,0,1,2:T(1,128)S(1)}, f32[1,4,192,512]{3,0,1,2:T(1,128)S(1)}, f32[192,4,1,512]{3,2,1,0:T(1,128)}) fusion(f32[192,4,2,512]{3,2,1,0:T(2,128)} %reshape.55, s32[]{:T(128)S(6)} %select_n.335, s32[]{:T(128)S(6)} %select_n.336, f32[192,4,2,512]{3,2,1,0:T(2,128)} %reshape.54), kind=kLoop, calls=%fused_computation.273 | loop fusion | bytes 12582920 | tf_op jit(solution)/shard_map/dynamic-slice.2
  187.6 21.7 %fusion.4 = f32[192,4096]{1,0:T(8,128)} fusion(f32[4096,2048]{1,0:T(8,128)} %param.9, f32[192,2048]{1,0:T(8,128)} %constant_dynamic-update-slice_fusion.4, f32[192,2048]{1,0:T(8,128)S(1)} %constant_dynamic-update-slice_fusion, f32[192,2048]{1,0:T(8,128)S(1)} %constant_dynamic-update-slice_fusion.2, pred[]{:T(512)S(6)} %eq.32, pred[]{:T(512)S(6)} %eq.31), kind=kOutput, calls=%fused_computation.18 | convolution fusion | flops 9664462848 | bytes 41418752 | tf_op jit(solution)/shard_map/dot_general | solution.py:21
  209.3 21.9 %fusion.7 = f32[192,4096]{1,0:T(8,128)} fusion(f32[4096,2048]{1,0:T(8,128)} %param.9, f32[192,2048]{1,0:T(8,128)} %constant_dynamic-update-slice_fusion.4, f32[192,2048]{1,0:T(8,128)S(1)} %constant_dynamic-update-slice_fusion, pred[]{:T(512)S(6)} %eq.30), kind=kOutput, calls=%fused_computation.22 | convolution fusion | flops 9664069632 | bytes 39845888 | tf_op jit(solution)/shard_map/dot_general | solution.py:21
  231.2 4.2 reshape.57
  235.4 5.7 %reshape.56 = f32[192,4,2,512]{3,2,1,0:T(2,128)} reshape(f32[192,4096]{1,0:T(8,128)} %fusion.7) | data formatting | bytes 6291456 | tf_op jit(solution)/shard_map/reshape | solution.py:150
  241.2 11.0 %constant_dynamic-slice_fusion.16 = (f32[192,4,1,512]{3,2,1,0:T(1,128)S(1)}, f32[1,4,192,512]{3,0,1,2:T(1,128)}, f32[1,4,192,512]{3,0,1,2:T(1,128)}, f32[192,4,1,512]{3,2,1,0:T(1,128)S(1)}) fusion(f32[192,4,2,512]{3,2,1,0:T(2,128)S(1)} %reshape.57, s32[]{:T(128)S(6)} %select_n.335, s32[]{:T(128)S(6)} %select_n.336, f32[192,4,2,512]{3,2,1,0:T(2,128)} %reshape.56), kind=kLoop, calls=%fused_computation.257 | loop fusion | bytes 12582920 | tf_op jit(solution)/shard_map/dynamic-slice.6
  260.8 10.3 %collective-permute-start.1 = (f32[192,512]{1,0:T(8,128)S(1)}, f32[192,512]{1,0:T(8,128)S(1)}, u32[]{:S(2)}, u32[]{:S(2)}) collective-permute-start(f32[192,512]{1,0:T(8,128)S(1)} %bitcast.366), channel_id=1, source_target_pairs={{0,2},{1,3},{8,10},{9,11},{16,18},{17,19},{24,26},{25,27}} | collective-permute-start | bytes 1179656 | tf_op jit(solution)/shard_map/ppermute | solution.py:159
  277.6 2.7 collective-permute-done.1
  281.0 5.0 collective-permute-start.2
  286.1 2.6 collective-permute-done.12
  289.5 8.7 %collective-permute-start.13 = (f32[192,512]{1,0:T(8,128)S(1)}, f32[192,512]{1,0:T(8,128)S(1)}, u32[]{:S(2)}, u32[]{:S(2)}) collective-permute-start(f32[192,512]{1,0:T(8,128)S(1)} %bitcast_add_fusion.15), channel_id=1, source_target_pairs={{0,2},{1,3},{2,4},{3,5},{8,10},{9,11},{10,12},{11,13},{16,18},{17,... | collective-permute-start | bytes 1179656 | tf_op jit(solution)/shard_map/ppermute | solution.py:159
  299.6 9.1 %collective-permute-start.3 = (f32[192,512]{1,0:T(8,128)S(1)}, f32[192,512]{1,0:T(8,128)S(1)}, u32[]{:S(2)}, u32[]{:S(2)}) collective-permute-start(f32[192,512]{1,0:T(8,128)S(1)} %bitcast_add_fusion.21), channel_id=1, source_target_pairs={{0,2},{1,3},{2,4},{3,5},{4,6},{5,7},{8,10},{9,11},{10,12},{11,13},... | collective-permute-start | bytes 1179656 | tf_op jit(solution)/shard_map/ppermute | solution.py:159
  314.5 3.3 constant_dynamic-slice_fusion.15
  317.9 5.5 %collective-permute-start.21 = (f32[192,512]{1,0:T(8,128)S(1)}, f32[192,512]{1,0:T(8,128)S(1)}, u32[]{:S(2)}, u32[]{:S(2)}) collective-permute-start(f32[192,512]{1,0:T(8,128)S(1)} %bitcast.365), channel_id=1, source_target_pairs={{0,2},{1,3},{8,10},{9,11},{16,18},{17,19},{24,26},{25,27}} | collective-permute-start | bytes 1179656 | tf_op jit(solution)/shard_map/ppermute | solution.py:159
  324.2 6.7 %collective-permute-done.21 = f32[192,512]{1,0:T(8,128)S(1)} collective-permute-done((f32[192,512]{1,0:T(8,128)S(1)}, f32[192,512]{1,0:T(8,128)S(1)}, u32[]{:S(2)}, u32[]{:S(2)}) %collective-permute-start.21) | collective-permute-done | bytes 393248 | tf_op jit(solution)/shard_map/ppermute | solution.py:159
  330.9 4.4 collective-permute-start.28
  336.8 8.1 %collective-permute-done.28 = f32[192,512]{1,0:T(8,128)S(1)} collective-permute-done((f32[192,512]{1,0:T(8,128)S(1)}, f32[192,512]{1,0:T(8,128)S(1)}, u32[]{:S(2)}, u32[]{:S(2)}) %collective-permute-start.28) | collective-permute-done | bytes 393248 | tf_op jit(solution)/shard_map/ppermute | solution.py:159
  345.6 6.6 %collective-permute-start.22 = (f32[192,512]{1,0:T(8,128)S(1)}, f32[192,512]{1,0:T(8,128)S(1)}, u32[]{:S(2)}, u32[]{:S(2)}) collective-permute-start(f32[192,512]{1,0:T(8,128)S(1)} %bitcast_add_fusion.10), channel_id=1, source_target_pairs={{0,2},{1,3},{2,4},{3,5},{8,10},{9,11},{10,12},{11,13},{16,18},{17,... | collective-permute-start | bytes 1179656 | tf_op jit(solution)/shard_map/ppermute | solution.py:159
  353.3 5.2 collective-permute-start.29
  364.7 5.2 collective-permute-start.23
  372.9 5.3 %collective-permute-start.30 = (f32[192,512]{1,0:T(8,128)}, f32[192,512]{1,0:T(8,128)}, u32[]{:S(2)}, u32[]{:S(2)}) collective-permute-start(f32[192,512]{1,0:T(8,128)} %bitcast_add_fusion.6), channel_id=1, source_target_pairs={{0,2},{1,3},{2,4},{3,5},{4,6},{5,7},{8,10},{9,11},{10,12},{11,13},... | collective-permute-start | bytes 1179656 | tf_op jit(solution)/shard_map/ppermute | solution.py:159
  392.2 6.7 %collective-permute-done.45 = f32[96,768]{1,0:T(8,128)S(1)} collective-permute-done((f32[96,768]{1,0:T(8,128)S(1)}, f32[96,768]{1,0:T(8,128)S(1)}, u32[]{:S(2)}, u32[]{:S(2)}) %collective-permute-start.45) | collective-permute-done | bytes 294944 | tf_op jit(solution)/shard_map/ppermute | solution.py:101
  399.6 4.9 collective-permute-done.46
  404.6 4.6 collective-permute-start.47
  411.5 4.7 collective-permute-start.48
  424.9 2.9 collective-permute-done.56
  432.8 7.2 %broadcast_in_dim.51 = f32[32,32,24,32]{3,2,1,0:T(8,128)} broadcast(f32[32,32,24]{2,1,0:T(8,128)S(1)} %copy.27), dimensions={0,1,2} | broadcast | bytes 3244032 | tf_op jit(solution)/shard_map/broadcast_in_dim | solution.py:84
  440.0 9.8 %reshape.59.leaf_ref = f32[32,32,768]{2,1,0:T(8,128)} reshape(f32[32,32,24,32]{3,2,1,0:T(8,128)} %broadcast_in_dim.51) | data formatting | bytes 6291456 | tf_op jit(solution)/shard_map/reshape | solution.py:84
  455.4 6.7 %shard_map.104 = f32[768,768]{1,0:T(8,128)S(1)} custom-call(f32[32,32,768]{2,1,0:T(8,128)S(1)} %copy-done, f32[768,768]{1,0:T(8,128)S(1)} %copy-done.1), custom_call_target="tpu_custom_call" | custom-call | flops 905969664 | bytes 9437184 | tf_op jit(solution)/shard_map/pallas_call | solution.py:85
  468.5 3.0 collective-permute-done.51
  471.7 3.5 fusion.101
  480.0 3.2 fusion.43
  486.2 2.7 select_select_fusion.2
  491.0 2.9 fusion.54
  501.5 2.9 fusion.56
  (338 shorter events, 175.9 us)
Async XLA Ops:
  3.4 115.2 %collective-permute-start.7 = (f32[96,2048]{1,0:T(8,128)}, f32[96,2048]{1,0:T(8,128)}, u32[]{:S(2)}, u32[]{:S(2)}) collective-permute-start(f32[96,2048]{1,0:T(8,128)} %get-tuple-element.70), channel_id=1, source_target_pairs={{0,16},{8,24},{16,0},{24,8},{1,17},{9,25},{17,1},{25,9},{2,18},{10... | collective-permute-start | bytes 2359304 | tf_op jit(solution)/shard_map/ppermute | solution.py:101
  6.4 115.0 %collective-permute-start.9 = (f32[96,2048]{1,0:T(8,128)}, f32[96,2048]{1,0:T(8,128)}, u32[]{:S(2)}, u32[]{:S(2)}) collective-permute-start(f32[96,2048]{1,0:T(8,128)} %get-tuple-element.70), channel_id=1, source_target_pairs={{0,8},{8,0},{16,24},{24,16},{1,9},{9,1},{17,25},{25,17},{2,10},{10... | collective-permute-start | bytes 2359304 | tf_op jit(solution)/shard_map/ppermute | solution.py:101
  11.1 51.5 %collective-permute-start.34 = (f32[192,256]{1,0:T(8,128)}, f32[192,256]{1,0:T(8,128)S(1)}, u32[]{:S(2)}, u32[]{:S(2)}) collective-permute-start(f32[192,256]{1,0:T(8,128)} %bitcast.350), channel_id=1, source_target_pairs={{0,1},{1,0},{2,3},{3,2},{4,5},{5,4},{6,7},{7,6},{8,9},{9,8},{10,11... | collective-permute-start | bytes 589832 | tf_op jit(solution)/shard_map/ppermute | solution.py:101
  11.1 54.0 %collective-permute-start.35 = (f32[192,256]{1,0:T(8,128)S(1)}, f32[192,256]{1,0:T(8,128)S(1)}, u32[]{:S(2)}, u32[]{:S(2)}) collective-permute-start(f32[192,256]{1,0:T(8,128)S(1)} %bitcast.372), channel_id=1, source_target_pairs={{0,2},{1,3},{2,0},{3,1},{4,6},{5,7},{6,4},{7,5},{8,10},{9,11},{10,... | collective-permute-start | bytes 589832 | tf_op jit(solution)/shard_map/ppermute | solution.py:101
  12.8 52.5 %collective-permute-start.36 = (f32[192,256]{1,0:T(8,128)S(1)}, f32[192,256]{1,0:T(8,128)S(1)}, u32[]{:S(2)}, u32[]{:S(2)}) collective-permute-start(f32[192,256]{1,0:T(8,128)S(1)} %bitcast.371), channel_id=1, source_target_pairs={{0,3},{1,2},{2,1},{3,0},{4,7},{5,6},{6,5},{7,4},{8,11},{9,10},{10,... | collective-permute-start | bytes 589832 | tf_op jit(solution)/shard_map/ppermute | solution.py:101
  62.5 21.5 %collective-permute-start.37 = (f32[192,256]{1,0:T(8,128)}, f32[192,256]{1,0:T(8,128)S(1)}, u32[]{:S(2)}, u32[]{:S(2)}) collective-permute-start(f32[192,256]{1,0:T(8,128)} %bitcast.376), channel_id=1, source_target_pairs={{0,4},{1,5},{2,6},{3,7},{4,0},{5,1},{6,2},{7,3},{8,12},{9,13},{10,... | collective-permute-start | bytes 589832 | tf_op jit(solution)/shard_map/ppermute | solution.py:101
  65.1 21.8 %collective-permute-start.38 = (f32[192,256]{1,0:T(8,128)S(1)}, f32[192,256]{1,0:T(8,128)S(1)}, u32[]{:S(2)}, u32[]{:S(2)}) collective-permute-start(f32[192,256]{1,0:T(8,128)S(1)} %bitcast.375), channel_id=1, source_target_pairs={{0,5},{1,4},{2,7},{3,6},{4,1},{5,0},{6,3},{7,2},{8,13},{9,12},{10,... | collective-permute-start | bytes 589832 | tf_op jit(solution)/shard_map/ppermute | solution.py:101
  65.3 21.7 %collective-permute-start.39 = (f32[192,256]{1,0:T(8,128)S(1)}, f32[192,256]{1,0:T(8,128)S(1)}, u32[]{:S(2)}, u32[]{:S(2)}) collective-permute-start(f32[192,256]{1,0:T(8,128)S(1)} %bitcast.374), channel_id=1, source_target_pairs={{0,6},{1,7},{2,4},{3,5},{4,2},{5,3},{6,0},{7,1},{8,14},{9,15},{10,... | collective-permute-start | bytes 589832 | tf_op jit(solution)/shard_map/ppermute | solution.py:101
  84.0 8.8 %collective-permute-start.40 = (f32[192,256]{1,0:T(8,128)S(1)}, f32[192,256]{1,0:T(8,128)S(1)}, u32[]{:S(2)}, u32[]{:S(2)}) collective-permute-start(f32[192,256]{1,0:T(8,128)S(1)} %bitcast.373), channel_id=1, source_target_pairs={{0,7},{1,6},{2,5},{3,4},{4,3},{5,2},{6,1},{7,0},{8,15},{9,14},{10,... | collective-permute-start | bytes 589832 | tf_op jit(solution)/shard_map/ppermute | solution.py:101
  94.5 20.7 %collective-permute-start.43 = (f32[192,512]{1,0:T(8,128)}, f32[192,512]{1,0:T(8,128)}, u32[]{:S(2)}, u32[]{:S(2)}) collective-permute-start(f32[192,512]{1,0:T(8,128)} %get-tuple-element.29), channel_id=1, source_target_pairs={{0,24},{8,16},{16,8},{24,0},{1,25},{9,17},{17,9},{25,1},{2,26},{10... | collective-permute-start | bytes 1179656 | tf_op jit(solution)/shard_map/ppermute | solution.py:101
  94.9 20.8 %collective-permute-start.42 = (f32[192,512]{1,0:T(8,128)}, f32[192,512]{1,0:T(8,128)}, u32[]{:S(2)}, u32[]{:S(2)}) collective-permute-start(f32[192,512]{1,0:T(8,128)} %get-tuple-element.30), channel_id=1, source_target_pairs={{0,16},{8,24},{16,0},{24,8},{1,17},{9,25},{17,1},{25,9},{2,18},{10... | collective-permute-start | bytes 1179656 | tf_op jit(solution)/shard_map/ppermute | solution.py:101
  96.5 19.8 %collective-permute-start.41 = (f32[192,512]{1,0:T(8,128)}, f32[192,512]{1,0:T(8,128)}, u32[]{:S(2)}, u32[]{:S(2)}) collective-permute-start(f32[192,512]{1,0:T(8,128)} %get-tuple-element.31), channel_id=1, source_target_pairs={{0,8},{8,0},{16,24},{24,16},{1,9},{9,1},{17,25},{25,17},{2,10},{10... | collective-permute-start | bytes 1179656 | tf_op jit(solution)/shard_map/ppermute | solution.py:101
  115.2 18.6 %collective-permute-start.8 = (f32[96,2048]{1,0:T(8,128)}, f32[96,2048]{1,0:T(8,128)S(1)}, u32[]{:S(2)}, u32[]{:S(2)}) collective-permute-start(f32[96,2048]{1,0:T(8,128)} %get-tuple-element.69), channel_id=1, source_target_pairs={{0,16},{8,24},{16,0},{24,8},{1,17},{9,25},{17,1},{25,9},{2,18},{10... | collective-permute-start | bytes 2359304 | tf_op jit(solution)/shard_map/ppermute | solution.py:101
  115.7 20.7 %collective-permute-start.10 = (f32[96,2048]{1,0:T(8,128)}, f32[96,2048]{1,0:T(8,128)S(1)}, u32[]{:S(2)}, u32[]{:S(2)}) collective-permute-start(f32[96,2048]{1,0:T(8,128)} %get-tuple-element.69), channel_id=1, source_target_pairs={{0,8},{8,0},{16,24},{24,16},{1,9},{9,1},{17,25},{25,17},{2,10},{10... | collective-permute-start | bytes 2359304 | tf_op jit(solution)/shard_map/ppermute | solution.py:101
  118.7 64.8 %collective-permute-start.18 = (f32[96,2048]{1,0:T(8,128)}, f32[96,2048]{1,0:T(8,128)}, u32[]{:S(2)}, u32[]{:S(2)}) collective-permute-start(f32[96,2048]{1,0:T(8,128)} %collective-permute-done.7), channel_id=1, source_target_pairs={{0,8},{8,0},{16,24},{24,16},{1,9},{9,1},{17,25},{25,17},{2,10},{10... | collective-permute-start | bytes 2359304 | tf_op jit(solution)/shard_map/ppermute | solution.py:101
  165.4 20.1 %collective-permute-start.19 = (f32[96,2048]{1,0:T(8,128)}, f32[96,2048]{1,0:T(8,128)}, u32[]{:S(2)}, u32[]{:S(2)}) collective-permute-start(f32[96,2048]{1,0:T(8,128)} %copy-done.26), channel_id=1, source_target_pairs={{0,16},{8,24},{16,0},{24,8},{1,17},{9,25},{17,1},{25,9},{2,18},{10... | collective-permute-start | bytes 2359304 | tf_op jit(solution)/shard_map/ppermute | solution.py:101
  181.4 73.8 %collective-permute-start = (f32[4,192,512]{2,0,1:T(4,128)}, f32[4,192,512]{2,0,1:T(4,128)}, u32[]{:S(2)}, u32[]{:S(2)}) collective-permute-start(f32[4,192,512]{2,0,1:T(4,128)} %bitcast.335), channel_id=1, source_target_pairs={{0,1},{1,0},{2,3},{3,2},{4,5},{5,4},{6,7},{7,6},{8,9},{9,8},{10,11... | collective-permute-start | bytes 4718600 | tf_op jit(solution)/shard_map/ppermute | solution.py:101
  182.9 88.2 %collective-permute-start.11 = (f32[4,192,512]{2,0,1:T(4,128)}, f32[4,192,512]{2,0,1:T(4,128)}, u32[]{:S(2)}, u32[]{:S(2)}) collective-permute-start(f32[4,192,512]{2,0,1:T(4,128)} %bitcast.334), channel_id=1, source_target_pairs={{0,1},{1,0},{2,3},{3,2},{4,5},{5,4},{6,7},{7,6},{8,9},{9,8},{10,11... | collective-permute-start | bytes 4718600 | tf_op jit(solution)/shard_map/ppermute | solution.py:101
  254.1 54.6 %collective-permute-start.20 = (f32[4,192,512]{2,0,1:T(4,128)S(1)}, f32[4,192,512]{2,0,1:T(4,128)S(1)}, u32[]{:S(2)}, u32[]{:S(2)}) collective-permute-start(f32[4,192,512]{2,0,1:T(4,128)S(1)} %bitcast.362), channel_id=1, source_target_pairs={{0,1},{1,0},{2,3},{3,2},{4,5},{5,4},{6,7},{7,6},{8,9},{9,8},{10,11... | collective-permute-start | bytes 4718600 | tf_op jit(solution)/shard_map/ppermute | solution.py:101
  254.7 58.5 %collective-permute-start.27 = (f32[4,192,512]{2,0,1:T(4,128)S(1)}, f32[4,192,512]{2,0,1:T(4,128)S(1)}, u32[]{:S(2)}, u32[]{:S(2)}) collective-permute-start(f32[4,192,512]{2,0,1:T(4,128)S(1)} %bitcast.361), channel_id=1, source_target_pairs={{0,1},{1,0},{2,3},{3,2},{4,5},{5,4},{6,7},{7,6},{8,9},{9,8},{10,11... | collective-permute-start | bytes 4718600 | tf_op jit(solution)/shard_map/ppermute | solution.py:101
  260.0 16.2 %collective-permute-start.4 = (f32[192,512]{1,0:T(8,128)S(1)}, f32[192,512]{1,0:T(8,128)S(1)}, u32[]{:S(2)}, u32[]{:S(2)}) collective-permute-start(f32[192,512]{1,0:T(8,128)S(1)} %bitcast.367), channel_id=1, source_target_pairs={{7,5},{6,4},{15,13},{14,12},{23,21},{22,20},{31,29},{30,28}} | collective-permute-start | bytes 1179656 | tf_op jit(solution)/shard_map/ppermute | solution.py:160
  260.8 19.4 %collective-permute-start.1 = (f32[192,512]{1,0:T(8,128)S(1)}, f32[192,512]{1,0:T(8,128)S(1)}, u32[]{:S(2)}, u32[]{:S(2)}) collective-permute-start(f32[192,512]{1,0:T(8,128)S(1)} %bitcast.366), channel_id=1, source_target_pairs={{0,2},{1,3},{8,10},{9,11},{16,18},{17,19},{24,26},{25,27}} | collective-permute-start | bytes 1179656 | tf_op jit(solution)/shard_map/ppermute | solution.py:159
  276.2 12.5 %collective-permute-start.12 = (f32[192,512]{1,0:T(8,128)S(1)}, f32[192,512]{1,0:T(8,128)S(1)}, u32[]{:S(2)}, u32[]{:S(2)}) collective-permute-start(f32[192,512]{1,0:T(8,128)S(1)} %bitcast.369), channel_id=1, source_target_pairs={{0,2},{1,3},{8,10},{9,11},{16,18},{17,19},{24,26},{25,27}} | collective-permute-start | bytes 1179656 | tf_op jit(solution)/shard_map/ppermute | solution.py:159
  280.3 9.2 %collective-permute-start.5 = (f32[192,512]{1,0:T(8,128)S(1)}, f32[192,512]{1,0:T(8,128)S(1)}, u32[]{:S(2)}, u32[]{:S(2)}) collective-permute-start(f32[192,512]{1,0:T(8,128)S(1)} %bitcast_add_fusion.18), channel_id=1, source_target_pairs={{7,5},{6,4},{5,3},{4,2},{15,13},{14,12},{13,11},{12,10},{23,21},{2... | collective-permute-start | bytes 1179656 | tf_op jit(solution)/shard_map/ppermute | solution.py:160
  281.0 17.2 %collective-permute-start.2 = (f32[192,512]{1,0:T(8,128)S(1)}, f32[192,512]{1,0:T(8,128)S(1)}, u32[]{:S(2)}, u32[]{:S(2)}) collective-permute-start(f32[192,512]{1,0:T(8,128)S(1)} %bitcast_add_fusion.20), channel_id=1, source_target_pairs={{0,2},{1,3},{2,4},{3,5},{8,10},{9,11},{10,12},{11,13},{16,18},{17,... | collective-permute-start | bytes 1179656 | tf_op jit(solution)/shard_map/ppermute | solution.py:159
  288.7 10.9 %collective-permute-start.16 = (f32[192,512]{1,0:T(8,128)S(1)}, f32[192,512]{1,0:T(8,128)S(1)}, u32[]{:S(2)}, u32[]{:S(2)}) collective-permute-start(f32[192,512]{1,0:T(8,128)S(1)} %bitcast_add_fusion.13), channel_id=1, source_target_pairs={{7,5},{6,4},{5,3},{4,2},{15,13},{14,12},{13,11},{12,10},{23,21},{2... | collective-permute-start | bytes 1179656 | tf_op jit(solution)/shard_map/ppermute | solution.py:160
  289.5 28.4 %collective-permute-start.13 = (f32[192,512]{1,0:T(8,128)S(1)}, f32[192,512]{1,0:T(8,128)S(1)}, u32[]{:S(2)}, u32[]{:S(2)}) collective-permute-start(f32[192,512]{1,0:T(8,128)S(1)} %bitcast_add_fusion.15), channel_id=1, source_target_pairs={{0,2},{1,3},{2,4},{3,5},{8,10},{9,11},{10,12},{11,13},{16,18},{17,... | collective-permute-start | bytes 1179656 | tf_op jit(solution)/shard_map/ppermute | solution.py:159
  298.2 47.3 %collective-permute-start.6 = (f32[192,512]{1,0:T(8,128)S(1)}, f32[192,512]{1,0:T(8,128)S(1)}, u32[]{:S(2)}, u32[]{:S(2)}) collective-permute-start(f32[192,512]{1,0:T(8,128)S(1)} %bitcast_add_fusion.19), channel_id=1, source_target_pairs={{7,5},{6,4},{5,3},{4,2},{3,1},{2,0},{15,13},{14,12},{13,11},{12,10... | collective-permute-start | bytes 1179656 | tf_op jit(solution)/shard_map/ppermute | solution.py:160
  299.6 52.6 %collective-permute-start.3 = (f32[192,512]{1,0:T(8,128)S(1)}, f32[192,512]{1,0:T(8,128)S(1)}, u32[]{:S(2)}, u32[]{:S(2)}) collective-permute-start(f32[192,512]{1,0:T(8,128)S(1)} %bitcast_add_fusion.21), channel_id=1, source_target_pairs={{0,2},{1,3},{2,4},{3,5},{4,6},{5,7},{8,10},{9,11},{10,12},{11,13},... | collective-permute-start | bytes 1179656 | tf_op jit(solution)/shard_map/ppermute | solution.py:159
  308.8 44.5 %collective-permute-start.17 = (f32[192,512]{1,0:T(8,128)S(1)}, f32[192,512]{1,0:T(8,128)S(1)}, u32[]{:S(2)}, u32[]{:S(2)}) collective-permute-start(f32[192,512]{1,0:T(8,128)S(1)} %bitcast_add_fusion.14), channel_id=1, source_target_pairs={{7,5},{6,4},{5,3},{4,2},{3,1},{2,0},{15,13},{14,12},{13,11},{12,10... | collective-permute-start | bytes 1179656 | tf_op jit(solution)/shard_map/ppermute | solution.py:160
  313.1 10.3 %collective-permute-start.24 = (f32[192,512]{1,0:T(8,128)S(1)}, f32[192,512]{1,0:T(8,128)S(1)}, u32[]{:S(2)}, u32[]{:S(2)}) collective-permute-start(f32[192,512]{1,0:T(8,128)S(1)} %bitcast.363), channel_id=1, source_target_pairs={{7,5},{6,4},{15,13},{14,12},{23,21},{22,20},{31,29},{30,28}} | collective-permute-start | bytes 1179656 | tf_op jit(solution)/shard_map/ppermute | solution.py:160
  317.9 13.0 %collective-permute-start.21 = (f32[192,512]{1,0:T(8,128)S(1)}, f32[192,512]{1,0:T(8,128)S(1)}, u32[]{:S(2)}, u32[]{:S(2)}) collective-permute-start(f32[192,512]{1,0:T(8,128)S(1)} %bitcast.365), channel_id=1, source_target_pairs={{0,2},{1,3},{8,10},{9,11},{16,18},{17,19},{24,26},{25,27}} | collective-permute-start | bytes 1179656 | tf_op jit(solution)/shard_map/ppermute | solution.py:159
  323.4 11.9 %collective-permute-start.31 = (f32[192,512]{1,0:T(8,128)S(1)}, f32[192,512]{1,0:T(8,128)S(1)}, u32[]{:S(2)}, u32[]{:S(2)}) collective-permute-start(f32[192,512]{1,0:T(8,128)S(1)} %bitcast.368), channel_id=1, source_target_pairs={{7,5},{6,4},{15,13},{14,12},{23,21},{22,20},{31,29},{30,28}} | collective-permute-start | bytes 1179656 | tf_op jit(solution)/shard_map/ppermute | solution.py:160
  330.9 13.9 %collective-permute-start.28 = (f32[192,512]{1,0:T(8,128)S(1)}, f32[192,512]{1,0:T(8,128)S(1)}, u32[]{:S(2)}, u32[]{:S(2)}) collective-permute-start(f32[192,512]{1,0:T(8,128)S(1)} %bitcast.364), channel_id=1, source_target_pairs={{0,2},{1,3},{8,10},{9,11},{16,18},{17,19},{24,26},{25,27}} | collective-permute-start | bytes 1179656 | tf_op jit(solution)/shard_map/ppermute | solution.py:159
  335.4 23.1 %collective-permute-start.14 = (f32[192,512]{1,0:T(8,128)S(1)}, f32[192,512]{1,0:T(8,128)S(1)}, u32[]{:S(2)}, u32[]{:S(2)}) collective-permute-start(f32[192,512]{1,0:T(8,128)S(1)} %bitcast_add_fusion.16), channel_id=1, source_target_pairs={{0,2},{1,3},{2,4},{3,5},{4,6},{5,7},{8,10},{9,11},{10,12},{11,13},... | collective-permute-start | bytes 1179656 | tf_op jit(solution)/shard_map/ppermute | solution.py:159
  344.8 18.5 %collective-permute-start.25 = (f32[192,512]{1,0:T(8,128)S(1)}, f32[192,512]{1,0:T(8,128)S(1)}, u32[]{:S(2)}, u32[]{:S(2)}) collective-permute-start(f32[192,512]{1,0:T(8,128)S(1)} %bitcast_add_fusion.8), channel_id=1, source_target_pairs={{7,5},{6,4},{5,3},{4,2},{15,13},{14,12},{13,11},{12,10},{23,21},{2... | collective-permute-start | bytes 1179656 | tf_op jit(solution)/shard_map/ppermute | solution.py:160
  345.6 19.1 %collective-permute-start.22 = (f32[192,512]{1,0:T(8,128)S(1)}, f32[192,512]{1,0:T(8,128)S(1)}, u32[]{:S(2)}, u32[]{:S(2)}) collective-permute-start(f32[192,512]{1,0:T(8,128)S(1)} %bitcast_add_fusion.10), channel_id=1, source_target_pairs={{0,2},{1,3},{2,4},{3,5},{8,10},{9,11},{10,12},{11,13},{16,18},{17,... | collective-permute-start | bytes 1179656 | tf_op jit(solution)/shard_map/ppermute | solution.py:159
  352.2 17.7 %collective-permute-start.32 = (f32[192,512]{1,0:T(8,128)S(1)}, f32[192,512]{1,0:T(8,128)S(1)}, u32[]{:S(2)}, u32[]{:S(2)}) collective-permute-start(f32[192,512]{1,0:T(8,128)S(1)} %bitcast_add_fusion.3), channel_id=1, source_target_pairs={{7,5},{6,4},{5,3},{4,2},{15,13},{14,12},{13,11},{12,10},{23,21},{2... | collective-permute-start | bytes 1179656 | tf_op jit(solution)/shard_map/ppermute | solution.py:160
  353.3 18.8 %collective-permute-start.29 = (f32[192,512]{1,0:T(8,128)S(1)}, f32[192,512]{1,0:T(8,128)S(1)}, u32[]{:S(2)}, u32[]{:S(2)}) collective-permute-start(f32[192,512]{1,0:T(8,128)S(1)} %bitcast_add_fusion.5), channel_id=1, source_target_pairs={{0,2},{1,3},{2,4},{3,5},{8,10},{9,11},{10,12},{11,13},{16,18},{17,... | collective-permute-start | bytes 1179656 | tf_op jit(solution)/shard_map/ppermute | solution.py:159
  363.4 14.8 %collective-permute-start.26 = (f32[192,512]{1,0:T(8,128)S(1)}, f32[192,512]{1,0:T(8,128)S(1)}, u32[]{:S(2)}, u32[]{:S(2)}) collective-permute-start(f32[192,512]{1,0:T(8,128)S(1)} %bitcast_add_fusion.9), channel_id=1, source_target_pairs={{7,5},{6,4},{5,3},{4,2},{3,1},{2,0},{15,13},{14,12},{13,11},{12,10... | collective-permute-start | bytes 1179656 | tf_op jit(solution)/shard_map/ppermute | solution.py:160
  364.7 13.5 %collective-permute-start.23 = (f32[192,512]{1,0:T(8,128)S(1)}, f32[192,512]{1,0:T(8,128)S(1)}, u32[]{:S(2)}, u32[]{:S(2)}) collective-permute-start(f32[192,512]{1,0:T(8,128)S(1)} %bitcast_add_fusion.11), channel_id=1, source_target_pairs={{0,2},{1,3},{2,4},{3,5},{4,6},{5,7},{8,10},{9,11},{10,12},{11,13},... | collective-permute-start | bytes 1179656 | tf_op jit(solution)/shard_map/ppermute | solution.py:159
  370.7 15.0 %collective-permute-start.33 = (f32[192,512]{1,0:T(8,128)}, f32[192,512]{1,0:T(8,128)}, u32[]{:S(2)}, u32[]{:S(2)}) collective-permute-start(f32[192,512]{1,0:T(8,128)} %bitcast_add_fusion.4), channel_id=1, source_target_pairs={{7,5},{6,4},{5,3},{4,2},{3,1},{2,0},{15,13},{14,12},{13,11},{12,10... | collective-permute-start | bytes 1179656 | tf_op jit(solution)/shard_map/ppermute | solution.py:160
  372.9 12.9 %collective-permute-start.30 = (f32[192,512]{1,0:T(8,128)}, f32[192,512]{1,0:T(8,128)}, u32[]{:S(2)}, u32[]{:S(2)}) collective-permute-start(f32[192,512]{1,0:T(8,128)} %bitcast_add_fusion.6), channel_id=1, source_target_pairs={{0,2},{1,3},{2,4},{3,5},{4,6},{5,7},{8,10},{9,11},{10,12},{11,13},... | collective-permute-start | bytes 1179656 | tf_op jit(solution)/shard_map/ppermute | solution.py:159
  389.4 9.5 %collective-permute-start.45 = (f32[96,768]{1,0:T(8,128)S(1)}, f32[96,768]{1,0:T(8,128)S(1)}, u32[]{:S(2)}, u32[]{:S(2)}) collective-permute-start(f32[96,768]{1,0:T(8,128)S(1)} %slice_select_fusion.1), channel_id=1, source_target_pairs={{0,8},{8,0},{16,24},{24,16},{1,9},{9,1},{17,25},{25,17},{2,10},{10... | collective-permute-start | bytes 884744 | tf_op jit(solution)/shard_map/ppermute | solution.py:101
  391.9 7.7 %collective-permute-start.53 = (f32[192,384]{1,0:T(8,128)S(1)}, f32[192,384]{1,0:T(8,128)S(1)}, u32[]{:S(2)}, u32[]{:S(2)}) collective-permute-start(f32[192,384]{1,0:T(8,128)S(1)} %slice_select_fusion), channel_id=1, source_target_pairs={{0,1},{1,0},{2,3},{3,2},{4,5},{5,4},{6,7},{7,6},{8,9},{9,8},{10,11... | collective-permute-start | bytes 884744 | tf_op jit(solution)/shard_map/ppermute | solution.py:101
  411.5 7.7 %collective-permute-start.48 = (f32[24,768]{1,0:T(8,128)S(1)}, f32[24,768]{1,0:T(8,128)S(1)}, u32[]{:S(2)}, u32[]{:S(2)}) collective-permute-start(f32[24,768]{1,0:T(8,128)S(1)} %select_add_fusion.4), channel_id=1, source_target_pairs={{0,4},{1,5},{2,6},{3,7},{4,0},{5,1},{6,2},{7,3},{8,12},{9,13},{10,... | collective-permute-start | bytes 221192 | tf_op jit(solution)/shard_map/ppermute | solution.py:101
  424.4 39.4 %collective-permute-start.50 = (f32[48,768]{1,0:T(8,128)}, f32[48,768]{1,0:T(8,128)}, u32[]{:S(2)}, u32[]{:S(2)}) collective-permute-start(f32[48,768]{1,0:T(8,128)} %pad_maximum_fusion.6), channel_id=1, source_target_pairs={{0,16},{8,24},{16,0},{24,8},{1,17},{9,25},{17,1},{25,9},{2,18},{10... | collective-permute-start | bytes 442376 | tf_op jit(solution)/shard_map/ppermute | solution.py:101
  428.5 33.6 %collective-permute-start.57 = (f32[96,384]{1,0:T(8,128)}, f32[96,384]{1,0:T(8,128)}, u32[]{:S(2)}, u32[]{:S(2)}) collective-permute-start(f32[96,384]{1,0:T(8,128)} %add.361), channel_id=1, source_target_pairs={{0,4},{1,5},{2,6},{3,7},{4,0},{5,1},{6,2},{7,3},{8,12},{9,13},{10,... | collective-permute-start | bytes 442376 | tf_op jit(solution)/shard_map/ppermute | solution.py:101
  (54 other events, 659.2 us)
